TPU v7x, 32 devices: a whole 2x2x4 slice. The times are simulated.
32 devices in a mesh: section: 2 (over y), dp: 4 (over z), tensor: 4 (over x, core).
Axes of the slice: x: 2, y: 2, z: 4, core: 2. Of those that a mesh axis runs over, the one named last changes fastest.
Arguments:
- layer_input: bfloat16 [2, 2, 256, 8192], P('section', None, 'tensor', 'dp'), may hold values from -64 to 64
- ready_grad: bfloat16 [2, 256, 8192], P('section', 'tensor', 'dp'), may hold values from -6 to 6
- late_grad: bfloat16 [256, 8192], P('tensor', 'dp'), may hold values from -6 to 6
- norm_gain: float32 [2, 8192], P('section', 'dp'), may hold values from 0.25 to 4.5
- norm_bias: float32 [2, 8192], P('section', 'dp'), may hold values from -3 to 3
- up_weight: bfloat16 [2, 8192, 16384], P('section', 'dp', 'tensor'), may hold values from -0.0625 to 0.0625
- down_weight: bfloat16 [2, 16384, 8192], P('section', 'tensor', 'dp'), may hold values from -0.046875 to 0.046875
Outputs:
- input_grad: bfloat16 [2, 2, 256, 8192], P('section', None, 'tensor', 'dp')
- up_grad: bfloat16 [2, 8192, 16384], P('section', 'dp', 'tensor')
- down_grad: bfloat16 [2, 16384, 8192], P('section', 'tensor', 'dp')
- gain_grad: float32 [2, 8192], P('section', 'dp')
- bias_grad: float32 [2, 8192], P('section', 'dp')
All inputs are finite; a program needn't handle non-finite values.
Results may differ from a plain program's by a relative error of at most 0.03.
Values may be sent and summed in bfloat16 or wider, within the bound.
A program may use at most 192 MiB of HBM per device.

v0:
```python
import math
import jax
import jax.numpy as jnp
from jax import lax
from jax.sharding import PartitionSpec as P

MODEL_WIDTH = 8192
epsilon = 1e-05
inv_root_two = 0.7071067811865476
inv_root_two_pi = 0.3989422804014327


def from_behind(block, axis, distance):
    devices = range(lax.axis_size(axis))
    route = [(i - distance, i) for i in devices if i - distance in devices]
    return lax.ppermute(block, axis, route)


def gelu_value(values):
    return 0.5 * values * (1.0 + lax.erf(values * inv_root_two))


def gelu_slope(values):
    return (
        0.5 * (1.0 + lax.erf(values * inv_root_two))
        + values * jnp.exp(-0.5 * values * values) * inv_root_two_pi
    )


def round_partial(partial_value):
    return lax.optimization_barrier(partial_value.astype(jnp.bfloat16)).astype(jnp.float32)


def section_pass(inputs_tile, incoming_gradient, scale_gain, shift_bias, weight_up, weight_down):
    tensor_rows = inputs_tile.shape[0]
    inputs_float = inputs_tile.astype(jnp.float32)
    row_total, row_squares = lax.psum(
        (
            jnp.sum(inputs_float, axis=1, keepdims=True),
            jnp.sum(inputs_float * inputs_float, axis=1, keepdims=True),
        ),
        "dp",
    )
    row_mean = row_total / MODEL_WIDTH
    variance = row_squares / MODEL_WIDTH - row_mean * row_mean
    inverse_deviation = lax.rsqrt(variance + epsilon)
    centered_input = (inputs_float - row_mean) * inverse_deviation
    normalized = (centered_input * scale_gain + shift_bias).astype(jnp.bfloat16)
    normed_all = lax.all_gather(normalized, "tensor", axis=0, tiled=True)
    left_rows = normed_all
    pre_rows = lax.psum_scatter(
        round_partial(jnp.dot(left_rows, weight_up, preferred_element_type=jnp.float32)).astype(
            jnp.bfloat16
        ),
        "dp",
        scatter_dimension=0,
        tiled=True,
    ).astype(jnp.float32)
    act_all = lax.all_gather(gelu_value(pre_rows).astype(jnp.bfloat16), "dp", axis=0, tiled=True)
    slope = gelu_slope(pre_rows)
    down_term = jnp.dot(act_all.T, incoming_gradient, preferred_element_type=jnp.float32)
    left_rows = incoming_gradient
    act_grad = lax.psum_scatter(
        round_partial(
            lax.dot_general(
                left_rows, weight_down, (((1,), (1,)), ((), ())), preferred_element_type=jnp.float32
            )
        ).astype(jnp.bfloat16),
        "dp",
        scatter_dimension=0,
        tiled=True,
    ).astype(jnp.float32)
    pre_grad = (act_grad * slope).astype(jnp.bfloat16)
    pre_grad_all = lax.all_gather(pre_grad, "dp", axis=0, tiled=True)
    up_term = jnp.dot(normed_all.T, pre_grad_all, preferred_element_type=jnp.float32)
    left_rows = pre_grad_all
    normalized_gradient = lax.psum_scatter(
        lax.dot_general(
            left_rows, weight_up, (((1,), (1,)), ((), ())), preferred_element_type=jnp.float32
        ).astype(jnp.bfloat16),
        "tensor",
        scatter_dimension=0,
        tiled=True,
    ).astype(jnp.float32)
    gain_product = jnp.sum(normalized_gradient * centered_input, axis=0)
    bias_term = jnp.sum(normalized_gradient, axis=0)
    centered_gradient = normalized_gradient * scale_gain
    centered_total, centered_cross = lax.psum(
        (
            jnp.sum(centered_gradient, axis=1, keepdims=True),
            jnp.sum(centered_gradient * centered_input, axis=1, keepdims=True),
        ),
        "dp",
    )
    local_rows = lax.dynamic_slice_in_dim(
        incoming_gradient, lax.axis_index("tensor") * tensor_rows, tensor_rows, 0
    ).astype(jnp.float32)
    final_output = local_rows + inverse_deviation * (
        centered_gradient
        - centered_total / MODEL_WIDTH
        - centered_input * (centered_cross / MODEL_WIDTH)
    )
    return (final_output.astype(jnp.bfloat16), down_term, up_term, gain_product, bias_term)


def body(layer_input, ready_grad, late_grad, norm_gain, norm_bias, up_weight, down_weight):
    early = lax.axis_index("section") == 0
    scale_gain = norm_gain[0]
    shift_bias = norm_bias[0]
    weight_up = up_weight[0]
    weight_down = down_weight[0]
    ready_whole, late_whole = (
        lax.all_gather(ready_grad[0], "tensor", axis=0, tiled=True),
        lax.all_gather(late_grad, "tensor", axis=0, tiled=True),
    )
    first_pass = section_pass(
        layer_input[0, 0], ready_whole, scale_gain, shift_bias, weight_up, weight_down
    )
    sent = first_pass[0]
    assembled = lax.all_gather(sent, "tensor", axis=0, tiled=True)
    arrived = from_behind(assembled, "section", -1)
    second_incoming = jnp.where(early, arrived, late_whole)
    second_pass = section_pass(
        layer_input[0, 1], second_incoming, scale_gain, shift_bias, weight_up, weight_down
    )
    scale = 1.0 / math.sqrt(2 * second_incoming.shape[0])
    down_part = ((first_pass[1] + second_pass[1]) * scale).astype(jnp.bfloat16)
    up_part = ((first_pass[2] + second_pass[2]) * scale).astype(jnp.bfloat16)
    gain_sum, bias_sum = lax.psum(
        (first_pass[3] + second_pass[3], first_pass[4] + second_pass[4]), "tensor"
    )
    results = jnp.stack([first_pass[0], second_pass[0]])
    return (
        results[None],
        up_part[None],
        down_part[None],
        (gain_sum * scale)[None],
        (bias_sum * scale)[None],
    )


def solution(mesh):
    in_specs = (
        P("section", None, "tensor", "dp"),
        P("section", "tensor", "dp"),
        P("tensor", "dp"),
        P("section", "dp"),
        P("section", "dp"),
        P("section", "dp", "tensor"),
        P("section", "tensor", "dp"),
    )
    out_specs = (
        P("section", None, "tensor", "dp"),
        P("section", "dp", "tensor"),
        P("section", "tensor", "dp"),
        P("section", "dp"),
        P("section", "dp"),
    )
    return jax.shard_map(body, mesh=mesh, in_specs=in_specs, out_specs=out_specs, check_vma=False)
```

profile of v0, /device:TPU:0, one launch (start us, length us, event | category | flops | bytes accessed | tf_op | source)
XLA Modules:
  0.0 594.6 jit_solution(13825570276484820397)
XLA Ops:
  7.2 0.0 all-gather.11.cloned.1.call-start
  7.2 1.1 fusion.63
  8.3 1.2 convert_reduce_fusion.3
  9.5 13.5 %all-reduce.3 = (f32[64,1]{0,1:T(1,128)S(1)}, f32[64,1]{0,1:T(1,128)S(1)}) all-reduce(f32[64,1]{0,1:T(1,128)S(1)} %bitcast.170, f32[64,1]{0,1:T(1,128)S(1)} %bitcast.167), channel_id=1, replica_groups=mesh['section'=2,'dp'=4,'tensor'=4] {'dp'}, use_global_device_ids=true, to_apply=%region_3.0 | all-reduce | flops 128 | bytes 1024 | tf_op jit(solution)/shard_map/psum | solution.py:37
  23.0 1.9 fusion.68
  24.9 0.0 all-gather.27.cloned.1.call-start
  24.9 0.7 all-gather.27.cloned.1.call-update
  25.6 0.0 reduce-scatter.9.cloned.1.call-start
  25.7 14.3 %all-gather.11.cloned.1.call-done = bf16[256,2048]{1,0:T(8,128)(2,1)} async-done(((bf16[64,2048]{1,0:T(8,128)(2,1)}), bf16[256,2048]{1,0:T(8,128)(2,1)}) %all-gather.11.cloned.1.call-update) | async-done | bytes 1048592 | tf_op jit(solution)/shard_map/all_gather | solution.py:49
  40.0 11.9 %fusion.20 = bf16[256,4096]{1,0:T(8,128)(2,1)} fusion(bf16[256,2048]{1,0:T(8,128)(2,1)} %all-gather.11.cloned.1.call-done, bf16[1,2048,4096]{2,1,0:T(8,128)(2,1)} %param.12), kind=kOutput, calls=%fused_computation.18 | convolution fusion | flops 4296015872 | bytes 19922944 | tf_op jit(solution)/shard_map/dot_general | solution.py:52
  51.9 0.0 reduce-scatter.7.cloned.1.call-start
  52.0 6.3 %all-gather.27.cloned.1.call-done = bf16[1,256,2048]{2,1,0:T(8,128)(2,1)} async-done(((bf16[1,64,2048]{2,1,0:T(8,128)(2,1)}), bf16[1,256,2048]{2,1,0:T(8,128)(2,1)}) %all-gather.27.cloned.1.call-update) | async-done | bytes 1048592 | tf_op jit(solution)/shard_map/all_gather | solution.py:113
  58.3 12.0 %fusion.14 = bf16[256,4096]{1,0:T(8,128)(2,1)} fusion(bf16[1,4096,2048]{2,1,0:T(8,128)(2,1)} %param.13, bf16[1,256,2048]{2,1,0:T(8,128)(2,1)} %all-gather.27.cloned.1.call-done), kind=kOutput, calls=%fused_computation.16 | convolution fusion | flops 4296015872 | bytes 19922944 | tf_op jit(solution)/shard_map/dot_general | solution.py:65
  70.3 0.0 all-gather.13.cloned.1.call-start
  70.3 34.7 %reduce-scatter.9.cloned.1.call-done = bf16[64,4096]{1,0:T(8,128)(2,1)} async-done(((bf16[256,4096]{1,0:T(8,128)(2,1)}), bf16[64,4096]{1,0:T(8,128)(2,1)}) %reduce-scatter.9.cloned.1.call-update) | async-done | bytes 524304 | tf_op jit(solution)/shard_map/reduce_scatter | solution.py:51
  105.1 46.0 %reduce-scatter.7.cloned.1.call-done = bf16[64,4096]{1,0:T(8,128)(2,1)} async-done(((bf16[256,4096]{1,0:T(8,128)(2,1)}), bf16[64,4096]{1,0:T(8,128)(2,1)}) %reduce-scatter.7.cloned.1.call-update) | async-done | bytes 524304 | tf_op jit(solution)/shard_map/reduce_scatter | solution.py:63
  151.1 2.7 fusion.40
  153.9 0.5 reduce-scatter.11.cloned.1.call-start
  154.4 44.9 %all-gather.13.cloned.1.call-done = bf16[256,4096]{1,0:T(8,128)(2,1)} async-done(((bf16[64,4096]{1,0:T(8,128)(2,1)}), bf16[256,4096]{1,0:T(8,128)(2,1)}) %all-gather.13.cloned.1.call-update) | async-done | bytes 2097168 | tf_op jit(solution)/shard_map/all_gather | solution.py:74
  199.3 11.9 %fusion.26 = bf16[256,2048]{1,0:T(8,128)(2,1)} fusion(bf16[256,4096]{1,0:T(8,128)(2,1)} %all-gather.13.cloned.1.call-done, bf16[1,2048,4096]{2,1,0:T(8,128)(2,1)} %param.12), kind=kOutput, calls=%fused_computation.20 | convolution fusion | flops 4295491584 | bytes 19922944 | tf_op jit(solution)/shard_map/dot_general | solution.py:78
  211.2 0.0 all-gather.19.cloned.1.call-start
  211.3 23.7 %reduce-scatter.11.cloned.1.call-done = bf16[64,2048]{1,0:T(8,128)(2,1)} async-done(((bf16[256,2048]{1,0:T(8,128)(2,1)}), bf16[64,2048]{1,0:T(8,128)(2,1)}) %reduce-scatter.11.cloned.1.call-update) | async-done | bytes 262160 | tf_op jit(solution)/shard_map/reduce_scatter | solution.py:77
  235.0 1.4 fusion.85
  236.4 11.7 %all-reduce.2 = (f32[64,1]{0,1:T(1,128)S(1)}, f32[64,1]{0,1:T(1,128)S(1)}, f32[64,1]{0,1:T(1,128)S(1)}, f32[64,1]{0,1:T(1,128)S(1)}) all-reduce(f32[64,1]{0,1:T(1,128)S(1)} %bitcast.163, f32[64,1]{0,1:T(1,128)S(1)} %bitcast.165, f32[64,1]{0,1:T(1,128)S(1)} %bitcast.164, ...), channel_id=1, replica_groups=mesh['section'=2,'dp'=4,'tensor'=4] {'dp'}, use_global_device_ids=true, to_apply=%region_14.15 | all-reduce | flops 256 | bytes 2048 | tf_op jit(solution)/shard_map/psum | solution.py:37
  248.1 2.1 fusion.72
  250.2 0.0 all-gather.15.cloned.1.call-start
  250.2 0.7 all-gather.15.cloned.1.call-update
  250.9 0.0 all-gather.17.cloned.1.call-start
  251.0 0.7 all-gather.17.cloned.1.call-update
  251.7 0.0 reduce-scatter.15.cloned.1.call-start
  251.7 12.6 %all-gather.19.cloned.1.call-done = bf16[256,2048]{1,0:T(8,128)(2,1)} async-done(((bf16[64,2048]{1,0:T(8,128)(2,1)}), bf16[256,2048]{1,0:T(8,128)(2,1)}) %all-gather.19.cloned.1.call-update) | async-done | bytes 1048592 | tf_op jit(solution)/shard_map/all_gather | solution.py:49
  264.3 11.9 %fusion.23 = bf16[256,4096]{1,0:T(8,128)(2,1)} fusion(bf16[256,2048]{1,0:T(8,128)(2,1)} %all-gather.19.cloned.1.call-done, bf16[1,2048,4096]{2,1,0:T(8,128)(2,1)} %param.12), kind=kOutput, calls=%fused_computation.19 | convolution fusion | flops 4296015872 | bytes 19922944 | tf_op jit(solution)/shard_map/dot_general | solution.py:52
  276.3 0.0 reduce-scatter.13.cloned.1.call-start
  276.3 6.4 %all-gather.15.cloned.1.call-done = bf16[256,2048]{1,0:T(8,128)(2,1)} async-done(((bf16[64,2048]{1,0:T(8,128)(2,1)}), bf16[256,2048]{1,0:T(8,128)(2,1)}) %all-gather.15.cloned.1.call-update) | async-done | bytes 1048592 | tf_op jit(solution)/shard_map/all_gather | solution.py:120
  282.7 1.5 collective-permute-start
  284.2 16.9 %all-gather.17.cloned.1.call-done = bf16[256,2048]{1,0:T(8,128)(2,1)} async-done(((bf16[64,2048]{1,0:T(8,128)(2,1)}), bf16[256,2048]{1,0:T(8,128)(2,1)}) %all-gather.17.cloned.1.call-update) | async-done | bytes 1048592 | tf_op jit(solution)/shard_map/all_gather | solution.py:114
  301.1 9.1 %collective-permute-done = bf16[256,2048]{1,0:T(8,128)(2,1)} collective-permute-done((bf16[256,2048]{1,0:T(8,128)(2,1)}, bf16[256,2048]{1,0:T(8,128)(2,1)}, u32[]{:S(2)}, u32[]{:S(2)}) %collective-permute-start) | collective-permute-done | bytes 1048608 | tf_op jit(solution)/shard_map/ppermute | solution.py:16
  310.2 1.4 broadcast_select_fusion
  311.6 18.1 %fusion.17 = bf16[256,4096]{1,0:T(8,128)(2,1)} fusion(bf16[256,2048]{1,0:T(8,128)(2,1)S(1)} %broadcast_select_fusion, bf16[1,4096,2048]{2,1,0:T(8,128)(2,1)} %param.13), kind=kOutput, calls=%fused_computation.17 | convolution fusion | flops 4296015872 | bytes 19922944 | tf_op jit(solution)/shard_map/dot_general | solution.py:65
  329.7 0.0 all-gather.23.cloned.1.call-start
  329.7 0.5 all-gather.23.cloned.1.call-update
  330.2 0.0 all-gather.21.cloned.1.call-start
  330.3 17.5 %reduce-scatter.15.cloned.1.call-done = bf16[64,4096]{1,0:T(8,128)(2,1)} async-done(((bf16[256,4096]{1,0:T(8,128)(2,1)}), bf16[64,4096]{1,0:T(8,128)(2,1)}) %reduce-scatter.15.cloned.1.call-update) | async-done | bytes 524304 | tf_op jit(solution)/shard_map/reduce_scatter | solution.py:51
  347.8 46.1 %reduce-scatter.13.cloned.1.call-done = bf16[64,4096]{1,0:T(8,128)(2,1)} async-done(((bf16[256,4096]{1,0:T(8,128)(2,1)}), bf16[64,4096]{1,0:T(8,128)(2,1)}) %reduce-scatter.13.cloned.1.call-update) | async-done | bytes 524304 | tf_op jit(solution)/shard_map/reduce_scatter | solution.py:63
  393.9 2.7 fusion.49
  396.7 0.0 all-gather.25.cloned.1.call-start
  396.7 0.5 all-gather.25.cloned.1.call-update
  397.3 0.0 reduce-scatter.17.cloned.1.call-start
  397.3 17.7 %fusion.88 = f32[2048,4096]{1,0:T(8,128)} fusion(bf16[256,2048]{1,0:T(8,128)(2,1)} %all-gather.11.cloned.1.call-done, bf16[256,4096]{1,0:T(8,128)(2,1)} %all-gather.13.cloned.1.call-done), kind=kOutput, calls=%fused_computation.110 | convolution fusion | flops 4294967296 | bytes 36700160 | tf_op jit(solution)/shard_map/dot_general | solution.py:75
  415.0 26.3 %all-gather.23.cloned.1.call-done = bf16[256,4096]{1,0:T(8,128)(2,1)} async-done(((bf16[64,4096]{1,0:T(8,128)(2,1)}), bf16[256,4096]{1,0:T(8,128)(2,1)}) %all-gather.23.cloned.1.call-update) | async-done | bytes 2097168 | tf_op jit(solution)/shard_map/all_gather | solution.py:59
  441.3 15.4 %fusion.51 = f32[4096,2048]{1,0:T(8,128)} fusion(bf16[256,4096]{1,0:T(8,128)(2,1)} %all-gather.23.cloned.1.call-done, bf16[1,256,2048]{2,1,0:T(8,128)(2,1)S(1)} %copy-done.2), kind=kOutput, calls=%fused_computation.51 | convolution fusion | flops 4294967296 | bytes 36700160 | tf_op jit(solution)/shard_map/dot_general | solution.py:61
  456.7 31.5 %all-gather.21.cloned.1.call-done = bf16[256,4096]{1,0:T(8,128)(2,1)} async-done(((bf16[64,4096]{1,0:T(8,128)(2,1)}), bf16[256,4096]{1,0:T(8,128)(2,1)}) %all-gather.21.cloned.1.call-update) | async-done | bytes 2097168 | tf_op jit(solution)/shard_map/all_gather | solution.py:74
  488.2 11.9 %fusion.29 = bf16[256,2048]{1,0:T(8,128)(2,1)} fusion(bf16[256,4096]{1,0:T(8,128)(2,1)} %all-gather.21.cloned.1.call-done, bf16[1,2048,4096]{2,1,0:T(8,128)(2,1)} %param.12), kind=kOutput, calls=%fused_computation.21 | convolution fusion | flops 4295491584 | bytes 19922944 | tf_op jit(solution)/shard_map/dot_general | solution.py:78
  500.2 17.7 %fusion = bf16[1,2048,4096]{2,1,0:T(8,128)(2,1)} fusion(f32[2048,4096]{1,0:T(8,128)} %fusion.88, bf16[256,2048]{1,0:T(8,128)(2,1)S(1)} %copy-done.3, bf16[256,4096]{1,0:T(8,128)(2,1)} %all-gather.21.cloned.1.call-done), kind=kOutput, calls=%fused_computation.2 | convolution fusion | flops 4320133120 | bytes 53477376 | tf_op jit(solution)/shard_map/dot_general | solution.py:75
  517.8 17.1 %all-gather.25.cloned.1.call-done = bf16[256,4096]{1,0:T(8,128)(2,1)} async-done(((bf16[64,4096]{1,0:T(8,128)(2,1)}), bf16[256,4096]{1,0:T(8,128)(2,1)}) %all-gather.25.cloned.1.call-update) | async-done | bytes 2097168 | tf_op jit(solution)/shard_map/all_gather | solution.py:59
  534.9 17.7 %fusion.1 = bf16[1,4096,2048]{2,1,0:T(8,128)(2,1)} fusion(f32[4096,2048]{1,0:T(8,128)} %fusion.51, bf16[256,4096]{1,0:T(8,128)(2,1)} %all-gather.25.cloned.1.call-done, bf16[256,2048]{1,0:T(8,128)(2,1)S(1)} %broadcast_select_fusion), kind=kOutput, calls=%fused_computation.3 | convolution fusion | flops 4320133120 | bytes 53477376 | tf_op jit(solution)/shard_map/dot_general | solution.py:61
  552.7 8.5 %reduce-scatter.17.cloned.1.call-done = bf16[64,2048]{1,0:T(8,128)(2,1)} async-done(((bf16[256,2048]{1,0:T(8,128)(2,1)}), bf16[64,2048]{1,0:T(8,128)(2,1)}) %reduce-scatter.17.cloned.1.call-update) | async-done | bytes 262160 | tf_op jit(solution)/shard_map/reduce_scatter | solution.py:77
  561.1 1.4 fusion.86
  562.5 11.7 %all-reduce.1 = (f32[64,1]{0,1:T(1,128)S(1)}, f32[64,1]{0,1:T(1,128)S(1)}) all-reduce(f32[64,1]{0,1:T(1,128)S(1)} %bitcast.168, f32[64,1]{0,1:T(1,128)S(1)} %bitcast.169), channel_id=1, replica_groups=mesh['section'=2,'dp'=4,'tensor'=4] {'dp'}, use_global_device_ids=true, to_apply=%region_21.22 | all-reduce | flops 128 | bytes 1024 | tf_op jit(solution)/shard_map/psum | solution.py:88
  574.2 10.3 %all-reduce = (f32[2048]{0:T(1024)S(1)}, f32[2048]{0:T(1024)S(1)}) all-reduce(f32[2048]{0:T(1024)S(1)} %add.105, f32[2048]{0:T(1024)S(1)} %add.106), channel_id=1, replica_groups=mesh['section'=2,'dp'=4,'tensor'=4] {'tensor'}, use_global_device_ids=true, to_apply=%region_24.25 | all-reduce | flops 4096 | bytes 32768 | tf_op jit(solution)/shard_map/psum | solution.py:129
  584.5 0.6 broadcast_multiply_fusion.1
  585.1 0.6 broadcast_multiply_fusion
  585.7 1.3 fusion.87
  587.0 0.8 maximum_bitcast_fusion
  (29 shorter events, 0.2 us)
Async XLA Ops:
  7.2 32.8 %all-gather.11.cloned.1.call-start = ((), (), s32[]{:S(2)}) async-start(), calls=%async_computation.7 | async-start | bytes 1310720 | tf_op jit(solution)/shard_map/all_gather | solution.py:49
  24.9 33.4 %all-gather.27.cloned.1.call-start = ((), (), s32[]{:S(2)}) async-start(), calls=%async_computation.20 | async-start | bytes 1310720 | tf_op jit(solution)/shard_map/all_gather | solution.py:113
  25.6 79.4 %reduce-scatter.9.cloned.1.call-start = ((), (), s32[]{:S(2)}) async-start(), calls=%async_computation.8 | async-start | bytes 2621440 | tf_op jit(solution)/shard_map/reduce_scatter | solution.py:51
  51.9 99.2 %reduce-scatter.7.cloned.1.call-start = ((), (), s32[]{:S(2)}) async-start(), calls=%async_computation.6 | async-start | bytes 2621440 | tf_op jit(solution)/shard_map/reduce_scatter | solution.py:63
  70.3 164.7 %copy-start = (bf16[1,2,64,2048]{3,2,1,0:T(8,128)(2,1)S(1)}, bf16[1,2,64,2048]{3,2,1,0:T(8,128)(2,1)}, u32[]{:S(2)}) copy-start(bf16[1,2,64,2048]{3,2,1,0:T(8,128)(2,1)} %param.7) | copy-start | bytes 1572868
  70.3 164.7 %copy-start.4 = (f32[1,2048]{1,0:T(1,128)S(1)}, f32[1,2048]{1,0:T(1,128)}, u32[]{:S(2)}) copy-start(f32[1,2048]{1,0:T(1,128)} %param.10) | copy-start | bytes 24580
  70.3 129.0 %all-gather.13.cloned.1.call-start = ((), (), s32[]{:S(2)}) async-start(), calls=%async_computation.9 | async-start | bytes 2621440 | tf_op jit(solution)/shard_map/all_gather | solution.py:74
  153.8 94.2 %copy-start.2 = (bf16[1,256,2048]{2,1,0:T(8,128)(2,1)S(1)}, bf16[1,256,2048]{2,1,0:T(8,128)(2,1)}, u32[]{:S(2)}) copy-start(bf16[1,256,2048]{2,1,0:T(8,128)(2,1)} %all-gather.27.cloned.1.call-done) | copy-start | bytes 3145732
  153.9 94.2 %copy-start.5 = (f32[1,2048]{1,0:T(1,128)S(1)}, f32[1,2048]{1,0:T(1,128)}, u32[]{:S(2)}) copy-start(f32[1,2048]{1,0:T(1,128)} %param.11) | copy-start | bytes 24580
  153.9 81.1 %reduce-scatter.11.cloned.1.call-start = ((), (), s32[]{:S(2)}) async-start(), calls=%async_computation.10 | async-start | bytes 1310720 | tf_op jit(solution)/shard_map/reduce_scatter | solution.py:77
  211.2 53.1 %all-gather.19.cloned.1.call-start = ((), (), s32[]{:S(2)}) async-start(), calls=%async_computation.14 | async-start | bytes 1310720 | tf_op jit(solution)/shard_map/all_gather | solution.py:49
  250.2 32.5 %all-gather.15.cloned.1.call-start = ((), (), s32[]{:S(2)}) async-start(), calls=%async_computation.11 | async-start | bytes 1310720 | tf_op jit(solution)/shard_map/all_gather | solution.py:120
  250.9 50.2 %all-gather.17.cloned.1.call-start = ((), (), s32[]{:S(2)}) async-start(), calls=%async_computation.12 | async-start | bytes 1310720 | tf_op jit(solution)/shard_map/all_gather | solution.py:114
  251.7 96.2 %reduce-scatter.15.cloned.1.call-start = ((), (), s32[]{:S(2)}) async-start(), calls=%async_computation.15 | async-start | bytes 2621440 | tf_op jit(solution)/shard_map/reduce_scatter | solution.py:51
  276.3 117.7 %reduce-scatter.13.cloned.1.call-start = ((), (), s32[]{:S(2)}) async-start(), calls=%async_computation.13 | async-start | bytes 2621440 | tf_op jit(solution)/shard_map/reduce_scatter | solution.py:63
  282.7 27.5 %collective-permute-start = (bf16[256,2048]{1,0:T(8,128)(2,1)}, bf16[256,2048]{1,0:T(8,128)(2,1)}, u32[]{:S(2)}, u32[]{:S(2)}) collective-permute-start(bf16[256,2048]{1,0:T(8,128)(2,1)} %all-gather.15.cloned.1.call-done), channel_id=1, source_target_pairs={{16,0},{17,1},{18,2},{19,3},{20,4},{21,5},{22,6},{23,7},{24,8},{25... | collective-permute-start | bytes 3145736 | tf_op jit(solution)/shard_map/ppermute | solution.py:16
  329.7 111.6 %all-gather.23.cloned.1.call-start = ((), (), s32[]{:S(2)}) async-start(), calls=%async_computation.18 | async-start | bytes 2621440 | tf_op jit(solution)/shard_map/all_gather | solution.py:59
  330.2 158.0 %all-gather.21.cloned.1.call-start = ((), (), s32[]{:S(2)}) async-start(), calls=%async_computation.16 | async-start | bytes 2621440 | tf_op jit(solution)/shard_map/all_gather | solution.py:74
  396.7 138.3 %all-gather.25.cloned.1.call-start = ((), (), s32[]{:S(2)}) async-start(), calls=%async_computation.19 | async-start | bytes 2621440 | tf_op jit(solution)/shard_map/all_gather | solution.py:59
  397.3 163.9 %reduce-scatter.17.cloned.1.call-start = ((), (), s32[]{:S(2)}) async-start(), calls=%async_computation.17 | async-start | bytes 1310720 | tf_op jit(solution)/shard_map/reduce_scatter | solution.py:77
  456.7 43.5 %copy-start.3 = (bf16[256,2048]{1,0:T(8,128)(2,1)S(1)}, bf16[256,2048]{1,0:T(8,128)(2,1)}, u32[]{:S(2)}) copy-start(bf16[256,2048]{1,0:T(8,128)(2,1)} %all-gather.19.cloned.1.call-done) | copy-start | bytes 3145732
  517.8 69.2 %copy-start.1 = (bf16[64,2048]{1,0:T(8,128)(2,1)S(1)}, bf16[64,2048]{1,0:T(8,128)(2,1)}, u32[]{:S(2)}) copy-start(bf16[64,2048]{1,0:T(8,128)(2,1)} %get-tuple-element.26) | copy-start | bytes 786436
Sparse Core Ops, SparseCore 0:
  25.0 14.9 all-gather.10
  41.5 16.7 all-gather.26
  61.2 43.8 reduce-scatter.8
  107.9 43.1 reduce-scatter.6
  154.0 45.2 all-gather.12
  211.3 23.5 reduce-scatter.10
  250.3 13.9 all-gather.18
  265.9 16.7 all-gather.14
  284.3 16.7 all-gather.16
  303.9 43.8 reduce-scatter.14
  350.7 43.1 reduce-scatter.12
  396.0 45.2 all-gather.22
  443.5 44.6 all-gather.20
  490.3 44.6 all-gather.24
  537.5 23.6 reduce-scatter.16
where the time goes:
time: 602 us; the launch traced here: 595 us
  waiting for transfers between devices  365 us (61%)
  matrix products  146 us (24%)
  blocking collectives  47.1 us (8%)
  other arithmetic  19.2 us (3%)
  between operations  14.3 us (2%)
    reduce_scatter x2, waiting for transfers between devices, section_pass(): lax.psum_scatter(round_partial(lax.dot_general(left_rows, weight_down, ((...  92.1 us
    all_gather x2, waiting for transfers between devices, section_pass(): pre_grad_all = lax.all_gather(pre_grad, 'dp', axis=0, tiled=True)  76.4 us
    reduce_scatter x2, waiting for transfers between devices, section_pass(): lax.psum_scatter(round_partial(jnp.dot(left_rows, weight_up, preferred_el...  52.3 us
    all_gather x2, waiting for transfers between devices, section_pass(): lax.all_gather(gelu_value(pre_rows).astype(jnp.bfloat16), 'dp', axis=0, t...  43.4 us
    dot_general x2, matrix products, section_pass(): jnp.dot(normed_all.T, pre_grad_all, preferred_element_type=jnp.float32)  35.3 us
    dot_general x2, matrix products, section_pass(): jnp.dot(act_all.T, incoming_gradient, preferred_element_type=jnp.float32)  33.1 us
    reduce_scatter x2, waiting for transfers between devices, section_pass(): lax.psum_scatter(lax.dot_general(left_rows, weight_up, (((1,), (1,)), (()...  32.2 us
    dot_general x2, matrix products, section_pass(): lax.dot_general(left_rows, weight_down, (((1,), (1,)), ((), ())), preferr...  30 us
  transfers between devices with their start and end apart: 16, of which 16 were waited for; matrix products, arithmetic and copies ran while one was open for 23% of the time, Pallas kernels for 0%

commit v1 on v0

--- a/solution.py
+++ b/solution.py
@@ -56,7 +56,17 @@
         scatter_dimension=0,
         tiled=True,
     ).astype(jnp.float32)
-    act_all = lax.all_gather(gelu_value(pre_rows).astype(jnp.bfloat16), "dp", axis=0, tiled=True)
+    array = gelu_value(pre_rows).astype(jnp.bfloat16)
+    ways = lax.axis_size("dp")
+    up = [(d, (d + 1) % ways) for d in range(ways)]
+    down = [(d, (d - 1) % ways) for d in range(ways)]
+    earlier, later = ([array], [array])
+    for _ in range(ways // 2):
+        earlier.append(lax.ppermute(earlier[-1], "dp", up))
+    for _ in range((ways - 1) // 2):
+        later.append(lax.ppermute(later[-1], "dp", down))
+    line = jnp.concatenate([*earlier[::-1], *later[1:]], axis=0)
+    act_all = jnp.roll(line, (lax.axis_index("dp") - ways // 2) * array.shape[0], axis=0)
     slope = gelu_slope(pre_rows)
     down_term = jnp.dot(act_all.T, incoming_gradient, preferred_element_type=jnp.float32)
     left_rows = incoming_gradient

time: 602 us -> 609 us (1.012)
  starting transfers between devices: 2.52 us -> 20.5 us
  waiting for transfers between devices: 365 us -> 352 us
  matrix products: 146 us -> 153 us
    ppermute x0 -> x6, waiting for transfers between devices: none -> 59.8 us  [the longest x2 35.9 us: section_pass(): later.append(lax.ppermute(later[-1], 'dp', down))]
    all_gather x2 -> x0, waiting for transfers between devices: 43.4 us -> none  [section_pass(): lax.all_gather(gelu_value(pre_rows).astype(jnp.bfloat16), 'dp', axis=0, t...]
    all_gather x2, waiting for transfers between devices: 76.4 us -> 44.8 us  [section_pass(): pre_grad_all = lax.all_gather(pre_grad, 'dp', axis=0, tiled=True)]
    ppermute x0 -> x6, starting transfers between devices: none -> 18 us  [the longest x4 10.3 us: section_pass(): earlier.append(lax.ppermute(earlier[-1], 'dp', up))]
    reduce_scatter x2, waiting for transfers between devices: 52.3 us -> 63.8 us  [section_pass(): lax.psum_scatter(round_partial(jnp.dot(left_rows, weight_up, preferred_el...]
    reduce_scatter x2, waiting for transfers between devices: 32.2 us -> 23.7 us  [section_pass(): lax.psum_scatter(lax.dot_general(left_rows, weight_up, (((1,), (1,)), (()...]
  transfers between devices with their start and end apart: 16 -> 20, of which waited for: 16 -> 15; matrix products, arithmetic and copies ran while one was open for 23% -> 24% of each run, Pallas kernels for 0% -> 0%
where the time goes in v1:
time: 609 us; the launch traced here: 601 us
  waiting for transfers between devices  352 us (58%)
  matrix products  153 us (25%)
  blocking collectives  43.7 us (7%)
  starting transfers between devices  20.5 us (3%)
  other arithmetic  17.7 us (3%)
  between operations  14.3 us (2%)
    reduce_scatter x2, waiting for transfers between devices, section_pass(): lax.psum_scatter(round_partial(lax.dot_general(left_rows, weight_down, ((...  92.2 us
    reduce_scatter x2, waiting for transfers between devices, section_pass(): lax.psum_scatter(round_partial(jnp.dot(left_rows, weight_up, preferred_el...  63.8 us
    all_gather x2, waiting for transfers between devices, section_pass(): pre_grad_all = lax.all_gather(pre_grad, 'dp', axis=0, tiled=True)  44.8 us
    dot_general x2, matrix products, section_pass(): jnp.dot(act_all.T, incoming_gradient, preferred_element_type=jnp.float32)  38.3 us
    dot_general x2, matrix products, section_pass(): jnp.dot(normed_all.T, pre_grad_all, preferred_element_type=jnp.float32)  37.3 us
    ppermute x2, waiting for transfers between devices, section_pass(): later.append(lax.ppermute(later[-1], 'dp', down))  35.9 us
    dot_general x2, matrix products, section_pass(): lax.dot_general(left_rows, weight_down, (((1,), (1,)), ((), ())), preferr...  30 us
    all_gather x2, waiting for transfers between devices, section_pass(): normed_all = lax.all_gather(normalized, 'tensor', axis=0, tiled=True)  26.9 us
  transfers between devices with their start and end apart: 20, of which 15 were waited for; matrix products, arithmetic and copies ran while one was open for 24% of the time, Pallas kernels for 0%

profile of v1, /device:TPU:0, one launch (start us, length us, event | category | flops | bytes accessed | tf_op | source)
XLA Modules:
  0.0 601.5 jit_solution(10761048125505678709)
XLA Ops:
  7.2 0.0 all-gather.9.cloned.1.call-start
  7.2 1.1 fusion.81
  8.3 1.2 convert_reduce_fusion.3
  9.5 13.5 %all-reduce.3 = (f32[64,1]{0,1:T(1,128)S(1)}, f32[64,1]{0,1:T(1,128)S(1)}) all-reduce(f32[64,1]{0,1:T(1,128)S(1)} %bitcast.168, f32[64,1]{0,1:T(1,128)S(1)} %bitcast.165), channel_id=1, replica_groups=mesh['section'=2,'dp'=4,'tensor'=4] {'dp'}, use_global_device_ids=true, to_apply=%region_3.0 | all-reduce | flops 128 | bytes 1024 | tf_op jit(solution)/shard_map/psum | solution.py:37
  23.0 1.9 fusion.86
  24.9 0.0 all-gather.21.cloned.1.call-start
  24.9 0.7 all-gather.21.cloned.1.call-update
  25.6 0.0 reduce-scatter.9.cloned.1.call-start
  25.7 14.3 %all-gather.9.cloned.1.call-done = bf16[256,2048]{1,0:T(8,128)(2,1)} async-done(((bf16[64,2048]{1,0:T(8,128)(2,1)}), bf16[256,2048]{1,0:T(8,128)(2,1)}) %all-gather.9.cloned.1.call-update) | async-done | bytes 1048592 | tf_op jit(solution)/shard_map/all_gather | solution.py:49
  40.0 11.9 %fusion.20 = bf16[256,4096]{1,0:T(8,128)(2,1)} fusion(bf16[256,2048]{1,0:T(8,128)(2,1)} %all-gather.9.cloned.1.call-done, bf16[1,2048,4096]{2,1,0:T(8,128)(2,1)} %param.14), kind=kOutput, calls=%fused_computation.18 | convolution fusion | flops 4296015872 | bytes 19922944 | tf_op jit(solution)/shard_map/dot_general | solution.py:52
  51.9 0.0 reduce-scatter.7.cloned.1.call-start
  52.0 6.3 %all-gather.21.cloned.1.call-done = bf16[1,256,2048]{2,1,0:T(8,128)(2,1)} async-done(((bf16[1,64,2048]{2,1,0:T(8,128)(2,1)}), bf16[1,256,2048]{2,1,0:T(8,128)(2,1)}) %all-gather.21.cloned.1.call-update) | async-done | bytes 1048592 | tf_op jit(solution)/shard_map/all_gather | solution.py:123
  58.3 12.0 %fusion.14 = bf16[256,4096]{1,0:T(8,128)(2,1)} fusion(bf16[1,4096,2048]{2,1,0:T(8,128)(2,1)} %param.15, bf16[1,256,2048]{2,1,0:T(8,128)(2,1)} %all-gather.21.cloned.1.call-done), kind=kOutput, calls=%fused_computation.16 | convolution fusion | flops 4296015872 | bytes 19922944 | tf_op jit(solution)/shard_map/dot_general | solution.py:75
  70.3 0.0 all-gather.11.cloned.1.call-start
  70.3 34.8 %reduce-scatter.9.cloned.1.call-done = bf16[64,4096]{1,0:T(8,128)(2,1)} async-done(((bf16[256,4096]{1,0:T(8,128)(2,1)}), bf16[64,4096]{1,0:T(8,128)(2,1)}) %reduce-scatter.9.cloned.1.call-update) | async-done | bytes 524304 | tf_op jit(solution)/shard_map/reduce_scatter | solution.py:51
  105.1 46.1 %reduce-scatter.7.cloned.1.call-done = bf16[64,4096]{1,0:T(8,128)(2,1)} async-done(((bf16[256,4096]{1,0:T(8,128)(2,1)}), bf16[64,4096]{1,0:T(8,128)(2,1)}) %reduce-scatter.7.cloned.1.call-update) | async-done | bytes 524304 | tf_op jit(solution)/shard_map/reduce_scatter | solution.py:73
  151.1 2.6 fusion.59
  153.8 0.6 reduce-scatter.11.cloned.1.call-start
  154.3 44.8 %all-gather.11.cloned.1.call-done = bf16[256,4096]{1,0:T(8,128)(2,1)} async-done(((bf16[64,4096]{1,0:T(8,128)(2,1)}), bf16[256,4096]{1,0:T(8,128)(2,1)}) %all-gather.11.cloned.1.call-update) | async-done | bytes 2097168 | tf_op jit(solution)/shard_map/all_gather | solution.py:84
  199.2 11.9 %fusion.26 = bf16[256,2048]{1,0:T(8,128)(2,1)} fusion(bf16[256,4096]{1,0:T(8,128)(2,1)} %all-gather.11.cloned.1.call-done, bf16[1,2048,4096]{2,1,0:T(8,128)(2,1)} %param.14), kind=kOutput, calls=%fused_computation.36 | convolution fusion | flops 4295491584 | bytes 19922944 | tf_op jit(solution)/shard_map/dot_general | solution.py:88
  211.1 0.0 all-gather.17.cloned.1.call-start
  211.1 23.7 %reduce-scatter.11.cloned.1.call-done = bf16[64,2048]{1,0:T(8,128)(2,1)} async-done(((bf16[256,2048]{1,0:T(8,128)(2,1)}), bf16[64,2048]{1,0:T(8,128)(2,1)}) %reduce-scatter.11.cloned.1.call-update) | async-done | bytes 262160 | tf_op jit(solution)/shard_map/reduce_scatter | solution.py:87
  234.8 1.4 fusion.103
  236.2 11.7 %all-reduce.2 = (f32[64,1]{0,1:T(1,128)S(1)}, f32[64,1]{0,1:T(1,128)S(1)}, f32[64,1]{0,1:T(1,128)S(1)}, f32[64,1]{0,1:T(1,128)S(1)}) all-reduce(f32[64,1]{0,1:T(1,128)S(1)} %bitcast.161, f32[64,1]{0,1:T(1,128)S(1)} %bitcast.163, f32[64,1]{0,1:T(1,128)S(1)} %bitcast.162, ...), channel_id=1, replica_groups=mesh['section'=2,'dp'=4,'tensor'=4] {'dp'}, use_global_device_ids=true, to_apply=%region_14.15 | all-reduce | flops 256 | bytes 2048 | tf_op jit(solution)/shard_map/psum | solution.py:37
  247.9 2.2 fusion.90
  250.1 0.0 all-gather.13.cloned.1.call-start
  250.2 0.7 all-gather.13.cloned.1.call-update
  250.9 0.0 all-gather.15.cloned.1.call-start
  250.9 0.7 all-gather.15.cloned.1.call-update
  251.6 0.0 reduce-scatter.15.cloned.1.call-start
  251.6 12.6 %all-gather.17.cloned.1.call-done = bf16[256,2048]{1,0:T(8,128)(2,1)} async-done(((bf16[64,2048]{1,0:T(8,128)(2,1)}), bf16[256,2048]{1,0:T(8,128)(2,1)}) %all-gather.17.cloned.1.call-update) | async-done | bytes 1048592 | tf_op jit(solution)/shard_map/all_gather | solution.py:49
  264.2 11.9 %fusion.23 = bf16[256,4096]{1,0:T(8,128)(2,1)} fusion(bf16[256,2048]{1,0:T(8,128)(2,1)} %all-gather.17.cloned.1.call-done, bf16[1,2048,4096]{2,1,0:T(8,128)(2,1)} %param.14), kind=kOutput, calls=%fused_computation.19 | convolution fusion | flops 4296015872 | bytes 19922944 | tf_op jit(solution)/shard_map/dot_general | solution.py:52
  276.2 0.0 reduce-scatter.13.cloned.1.call-start
  276.2 6.4 %all-gather.13.cloned.1.call-done = bf16[256,2048]{1,0:T(8,128)(2,1)} async-done(((bf16[64,2048]{1,0:T(8,128)(2,1)}), bf16[256,2048]{1,0:T(8,128)(2,1)}) %all-gather.13.cloned.1.call-update) | async-done | bytes 1048592 | tf_op jit(solution)/shard_map/all_gather | solution.py:130
  282.6 1.5 collective-permute-start
  284.1 16.9 %all-gather.15.cloned.1.call-done = bf16[256,2048]{1,0:T(8,128)(2,1)} async-done(((bf16[64,2048]{1,0:T(8,128)(2,1)}), bf16[256,2048]{1,0:T(8,128)(2,1)}) %all-gather.15.cloned.1.call-update) | async-done | bytes 1048592 | tf_op jit(solution)/shard_map/all_gather | solution.py:124
  301.0 9.0 %collective-permute-done = bf16[256,2048]{1,0:T(8,128)(2,1)S(1)} collective-permute-done((bf16[256,2048]{1,0:T(8,128)(2,1)}, bf16[256,2048]{1,0:T(8,128)(2,1)S(1)}, u32[]{:S(2)}, u32[]{:S(2)}) %collective-permute-start) | collective-permute-done | bytes 1048608 | tf_op jit(solution)/shard_map/ppermute | solution.py:16
  310.0 0.1 broadcast_select_fusion
  310.1 18.1 %fusion.17 = bf16[256,4096]{1,0:T(8,128)(2,1)} fusion(bf16[256,2048]{1,0:T(8,128)(2,1)S(1)} %broadcast_select_fusion, bf16[1,4096,2048]{2,1,0:T(8,128)(2,1)} %param.15), kind=kOutput, calls=%fused_computation.17 | convolution fusion | flops 4296015872 | bytes 19922944 | tf_op jit(solution)/shard_map/dot_general | solution.py:75
  328.2 0.0 all-gather.19.cloned.1.call-start
  328.3 1.6 collective-permute-start.1
  329.8 29.0 %reduce-scatter.15.cloned.1.call-done = bf16[64,4096]{1,0:T(8,128)(2,1)} async-done(((bf16[256,4096]{1,0:T(8,128)(2,1)}), bf16[64,4096]{1,0:T(8,128)(2,1)}) %reduce-scatter.15.cloned.1.call-update) | async-done | bytes 524304 | tf_op jit(solution)/shard_map/reduce_scatter | solution.py:51
  358.8 46.1 %reduce-scatter.13.cloned.1.call-done = bf16[64,4096]{1,0:T(8,128)(2,1)} async-done(((bf16[256,4096]{1,0:T(8,128)(2,1)}), bf16[64,4096]{1,0:T(8,128)(2,1)}) %reduce-scatter.13.cloned.1.call-update) | async-done | bytes 524304 | tf_op jit(solution)/shard_map/reduce_scatter | solution.py:73
  405.0 2.6 fusion.68
  407.5 0.0 all-gather.19.cloned.1.call-update
  407.6 0.0 reduce-scatter.17.cloned.1.call-start
  407.6 3.9 collective-permute-start.3
  411.5 3.8 collective-permute-start.6
  415.3 11.6 %collective-permute-done.4 = bf16[64,4096]{1,0:T(8,128)(2,1)S(1)} collective-permute-done((bf16[64,4096]{1,0:T(8,128)(2,1)S(1)}, bf16[64,4096]{1,0:T(8,128)(2,1)S(1)}, u32[]{:S(2)}, u32[]{:S(2)}) %collective-permute-start.4) | collective-permute-done | bytes 524320 | tf_op jit(solution)/shard_map/ppermute | solution.py:65
  426.9 8.7 %collective-permute-start.5 = (bf16[64,4096]{1,0:T(8,128)(2,1)S(1)}, bf16[64,4096]{1,0:T(8,128)(2,1)S(1)}, u32[]{:S(2)}, u32[]{:S(2)}) collective-permute-start(bf16[64,4096]{1,0:T(8,128)(2,1)S(1)} %collective-permute-done.4), channel_id=1, source_target_pairs={{0,4},{4,8},{8,12},{12,0},{1,5},{5,9},{9,13},{13,1},{2,6},{6,10},{... | collective-permute-start | bytes 1572872 | tf_op jit(solution)/shard_map/ppermute | solution.py:65
  435.7 17.7 %fusion.110 = f32[2048,4096]{1,0:T(8,128)} fusion(bf16[256,2048]{1,0:T(8,128)(2,1)} %all-gather.9.cloned.1.call-done, bf16[256,4096]{1,0:T(8,128)(2,1)} %all-gather.11.cloned.1.call-done), kind=kOutput, calls=%fused_computation.144 | convolution fusion | flops 4294967296 | bytes 36700160 | tf_op jit(solution)/shard_map/dot_general | solution.py:85
  453.4 35.9 %collective-permute-done.6 = bf16[64,4096]{1,0:T(8,128)(2,1)S(1)} collective-permute-done((bf16[64,4096]{1,0:T(8,128)(2,1)S(1)}, bf16[64,4096]{1,0:T(8,128)(2,1)S(1)}, u32[]{:S(2)}, u32[]{:S(2)}) %collective-permute-start.6) | collective-permute-done | bytes 524320 | tf_op jit(solution)/shard_map/ppermute | solution.py:67
  489.2 12.2 %collective-permute-done.5 = bf16[64,4096]{1,0:T(8,128)(2,1)S(1)} collective-permute-done((bf16[64,4096]{1,0:T(8,128)(2,1)S(1)}, bf16[64,4096]{1,0:T(8,128)(2,1)S(1)}, u32[]{:S(2)}, u32[]{:S(2)}) %collective-permute-start.5) | collective-permute-done | bytes 524320 | tf_op jit(solution)/shard_map/ppermute | solution.py:65
  501.5 16.0 %fusion.36 = f32[4096,2048]{1,0:T(8,128)} fusion(bf16[256,2048]{1,0:T(8,128)(2,1)S(1)} %broadcast_select_fusion, s32[]{:T(128)S(6)} %select_n.28, bf16[64,4096]{1,0:T(8,128)(2,1)S(1)} %collective-permute-done.5, bf16[64,4096]{1,0:T(8,128)(2,1)S(1)} %collective-permute-done.4, bf16[64,4096]{1,0:T(8,128)(2,1)S(1)} %get-tuple-element.31, ...), kind=kOutput, calls=%fused_computation.42 | convolution fusion | flops 4311744512 | bytes 36700164 | tf_op jit(solution)/shard_map/dot_general | solution.py:71
  517.5 12.0 %fusion.29 = bf16[256,2048]{1,0:T(8,128)(2,1)} fusion(bf16[256,4096]{1,0:T(8,128)(2,1)} %all-gather.19.cloned.1.call-done, bf16[1,2048,4096]{2,1,0:T(8,128)(2,1)} %param.14), kind=kOutput, calls=%fused_computation.37 | convolution fusion | flops 4295491584 | bytes 19922944 | tf_op jit(solution)/shard_map/dot_general | solution.py:88
  529.5 22.3 %fusion.1 = bf16[1,4096,2048]{2,1,0:T(8,128)(2,1)} fusion(f32[4096,2048]{1,0:T(8,128)} %fusion.36, s32[]{:T(128)S(6)} %select_n.28, bf16[64,4096]{1,0:T(8,128)(2,1)} %collective-permute-done.2, bf16[64,4096]{1,0:T(8,128)(2,1)} %collective-permute-done.1, bf16[64,4096]{1,0:T(8,128)(2,1)S(1)} %get-tuple-element.29, ...), kind=kOutput, calls=%fused_computation.3 | convolution fusion | flops 4336910336 | bytes 53477380 | tf_op jit(solution)/shard_map/dot_general | solution.py:71
  551.8 19.6 %fusion = bf16[1,2048,4096]{2,1,0:T(8,128)(2,1)} fusion(f32[2048,4096]{1,0:T(8,128)} %fusion.110, bf16[256,2048]{1,0:T(8,128)(2,1)} %all-gather.17.cloned.1.call-done, bf16[256,4096]{1,0:T(8,128)(2,1)} %all-gather.19.cloned.1.call-done), kind=kOutput, calls=%fused_computation.2 | convolution fusion | flops 4320133120 | bytes 53477376 | tf_op jit(solution)/shard_map/dot_general | solution.py:85
  571.4 1.4 fusion.104
  572.8 8.4 %all-reduce.1 = (f32[64,1]{0,1:T(1,128)S(1)}, f32[64,1]{0,1:T(1,128)S(1)}) all-reduce(f32[64,1]{0,1:T(1,128)S(1)} %bitcast.166, f32[64,1]{0,1:T(1,128)S(1)} %bitcast.167), channel_id=1, replica_groups=mesh['section'=2,'dp'=4,'tensor'=4] {'dp'}, use_global_device_ids=true, to_apply=%region_21.22 | all-reduce | flops 128 | bytes 1024 | tf_op jit(solution)/shard_map/psum | solution.py:98
  581.2 10.1 %all-reduce = (f32[2048]{0:T(1024)S(1)}, f32[2048]{0:T(1024)S(1)}) all-reduce(f32[2048]{0:T(1024)S(1)} %add.114, f32[2048]{0:T(1024)S(1)} %add.115), channel_id=1, replica_groups=mesh['section'=2,'dp'=4,'tensor'=4] {'tensor'}, use_global_device_ids=true, to_apply=%region_24.26 | all-reduce | flops 4096 | bytes 32768 | tf_op jit(solution)/shard_map/psum | solution.py:139
  591.3 0.6 broadcast_multiply_fusion.1
  591.9 0.6 broadcast_multiply_fusion
  592.5 1.3 fusion.105
  593.8 0.8 maximum_bitcast_fusion
  (33 shorter events, 0.2 us)
Async XLA Ops:
  7.2 32.8 %all-gather.9.cloned.1.call-start = ((), (), s32[]{:S(2)}) async-start(), calls=%async_computation.7 | async-start | bytes 1310720 | tf_op jit(solution)/shard_map/all_gather | solution.py:49
  24.9 33.4 %all-gather.21.cloned.1.call-start = ((), (), s32[]{:S(2)}) async-start(), calls=%async_computation.18 | async-start | bytes 1310720 | tf_op jit(solution)/shard_map/all_gather | solution.py:123
  25.6 79.4 %reduce-scatter.9.cloned.1.call-start = ((), (), s32[]{:S(2)}) async-start(), calls=%async_computation.8 | async-start | bytes 2621440 | tf_op jit(solution)/shard_map/reduce_scatter | solution.py:51
  51.9 99.2 %reduce-scatter.7.cloned.1.call-start = ((), (), s32[]{:S(2)}) async-start(), calls=%async_computation.6 | async-start | bytes 2621440 | tf_op jit(solution)/shard_map/reduce_scatter | solution.py:73
  70.3 128.9 %all-gather.11.cloned.1.call-start = ((), (), s32[]{:S(2)}) async-start(), calls=%async_computation.9 | async-start | bytes 2621440 | tf_op jit(solution)/shard_map/all_gather | solution.py:84
  153.7 81.1 %copy-start = (bf16[1,2,64,2048]{3,2,1,0:T(8,128)(2,1)S(1)}, bf16[1,2,64,2048]{3,2,1,0:T(8,128)(2,1)}, u32[]{:S(2)}) copy-start(bf16[1,2,64,2048]{3,2,1,0:T(8,128)(2,1)} %param.9) | copy-start | bytes 1572868
  153.7 81.1 %copy-start.3 = (f32[1,2048]{1,0:T(1,128)S(1)}, f32[1,2048]{1,0:T(1,128)}, u32[]{:S(2)}) copy-start(f32[1,2048]{1,0:T(1,128)} %param.12) | copy-start | bytes 24580
  153.8 94.2 %copy-start.4 = (f32[1,2048]{1,0:T(1,128)S(1)}, f32[1,2048]{1,0:T(1,128)}, u32[]{:S(2)}) copy-start(f32[1,2048]{1,0:T(1,128)} %param.13) | copy-start | bytes 24580
  153.8 81.1 %reduce-scatter.11.cloned.1.call-start = ((), (), s32[]{:S(2)}) async-start(), calls=%async_computation.10 | async-start | bytes 1310720 | tf_op jit(solution)/shard_map/reduce_scatter | solution.py:87
  211.1 53.2 %all-gather.17.cloned.1.call-start = ((), (), s32[]{:S(2)}) async-start(), calls=%async_computation.14 | async-start | bytes 1310720 | tf_op jit(solution)/shard_map/all_gather | solution.py:49
  250.1 32.5 %all-gather.13.cloned.1.call-start = ((), (), s32[]{:S(2)}) async-start(), calls=%async_computation.11 | async-start | bytes 1310720 | tf_op jit(solution)/shard_map/all_gather | solution.py:130
  250.9 50.2 %all-gather.15.cloned.1.call-start = ((), (), s32[]{:S(2)}) async-start(), calls=%async_computation.12 | async-start | bytes 1310720 | tf_op jit(solution)/shard_map/all_gather | solution.py:124
  251.6 107.2 %reduce-scatter.15.cloned.1.call-start = ((), (), s32[]{:S(2)}) async-start(), calls=%async_computation.15 | async-start | bytes 2621440 | tf_op jit(solution)/shard_map/reduce_scatter | solution.py:51
  276.2 128.8 %reduce-scatter.13.cloned.1.call-start = ((), (), s32[]{:S(2)}) async-start(), calls=%async_computation.13 | async-start | bytes 2621440 | tf_op jit(solution)/shard_map/reduce_scatter | solution.py:73
  282.6 27.4 %collective-permute-start = (bf16[256,2048]{1,0:T(8,128)(2,1)}, bf16[256,2048]{1,0:T(8,128)(2,1)S(1)}, u32[]{:S(2)}, u32[]{:S(2)}) collective-permute-start(bf16[256,2048]{1,0:T(8,128)(2,1)} %all-gather.13.cloned.1.call-done), channel_id=1, source_target_pairs={{16,0},{17,1},{18,2},{19,3},{20,4},{21,5},{22,6},{23,7},{24,8},{25... | collective-permute-start | bytes 3145736 | tf_op jit(solution)/shard_map/ppermute | solution.py:16
  328.2 189.2 %all-gather.19.cloned.1.call-start = ((), (), s32[]{:S(2)}) async-start(), calls=%async_computation.16 | async-start | bytes 2621440 | tf_op jit(solution)/shard_map/all_gather | solution.py:84
  328.3 83.2 %collective-permute-start.1 = (bf16[64,4096]{1,0:T(8,128)(2,1)S(1)}, bf16[64,4096]{1,0:T(8,128)(2,1)}, u32[]{:S(2)}, u32[]{:S(2)}) collective-permute-start(bf16[64,4096]{1,0:T(8,128)(2,1)S(1)} %get-tuple-element.29), channel_id=1, source_target_pairs={{0,4},{4,8},{8,12},{12,0},{1,5},{5,9},{9,13},{13,1},{2,6},{6,10},{... | collective-permute-start | bytes 1572872 | tf_op jit(solution)/shard_map/ppermute | solution.py:65
  407.5 19.4 %collective-permute-start.4 = (bf16[64,4096]{1,0:T(8,128)(2,1)S(1)}, bf16[64,4096]{1,0:T(8,128)(2,1)S(1)}, u32[]{:S(2)}, u32[]{:S(2)}) collective-permute-start(bf16[64,4096]{1,0:T(8,128)(2,1)S(1)} %get-tuple-element.31), channel_id=1, source_target_pairs={{0,4},{4,8},{8,12},{12,0},{1,5},{5,9},{9,13},{13,1},{2,6},{6,10},{... | collective-permute-start | bytes 1572872 | tf_op jit(solution)/shard_map/ppermute | solution.py:65
  407.6 163.9 %reduce-scatter.17.cloned.1.call-start = ((), (), s32[]{:S(2)}) async-start(), calls=%async_computation.17 | async-start | bytes 1310720 | tf_op jit(solution)/shard_map/reduce_scatter | solution.py:87
  407.6 121.9 %collective-permute-start.3 = (bf16[64,4096]{1,0:T(8,128)(2,1)S(1)}, bf16[64,4096]{1,0:T(8,128)(2,1)}, u32[]{:S(2)}, u32[]{:S(2)}) collective-permute-start(bf16[64,4096]{1,0:T(8,128)(2,1)S(1)} %get-tuple-element.29), channel_id=1, source_target_pairs={{0,12},{4,0},{8,4},{12,8},{1,13},{5,1},{9,5},{13,9},{2,14},{6,2},{... | collective-permute-start | bytes 1572872 | tf_op jit(solution)/shard_map/ppermute | solution.py:67
  411.5 118.0 %collective-permute-start.2 = (bf16[64,4096]{1,0:T(8,128)(2,1)}, bf16[64,4096]{1,0:T(8,128)(2,1)}, u32[]{:S(2)}, u32[]{:S(2)}) collective-permute-start(bf16[64,4096]{1,0:T(8,128)(2,1)} %collective-permute-done.1), channel_id=1, source_target_pairs={{0,4},{4,8},{8,12},{12,0},{1,5},{5,9},{9,13},{13,1},{2,6},{6,10},{... | collective-permute-start | bytes 1572872 | tf_op jit(solution)/shard_map/ppermute | solution.py:65
  411.5 77.7 %collective-permute-start.6 = (bf16[64,4096]{1,0:T(8,128)(2,1)S(1)}, bf16[64,4096]{1,0:T(8,128)(2,1)S(1)}, u32[]{:S(2)}, u32[]{:S(2)}) collective-permute-start(bf16[64,4096]{1,0:T(8,128)(2,1)S(1)} %get-tuple-element.31), channel_id=1, source_target_pairs={{0,12},{4,0},{8,4},{12,8},{1,13},{5,1},{9,5},{13,9},{2,14},{6,2},{... | collective-permute-start | bytes 1572872 | tf_op jit(solution)/shard_map/ppermute | solution.py:67
  426.9 74.5 %collective-permute-start.5 = (bf16[64,4096]{1,0:T(8,128)(2,1)S(1)}, bf16[64,4096]{1,0:T(8,128)(2,1)S(1)}, u32[]{:S(2)}, u32[]{:S(2)}) collective-permute-start(bf16[64,4096]{1,0:T(8,128)(2,1)S(1)} %collective-permute-done.4), channel_id=1, source_target_pairs={{0,4},{4,8},{8,12},{12,0},{1,5},{5,9},{9,13},{13,1},{2,6},{6,10},{... | collective-permute-start | bytes 1572872 | tf_op jit(solution)/shard_map/ppermute | solution.py:65
  517.5 12.1 %copy-start.2 = (bf16[1,256,2048]{2,1,0:T(8,128)(2,1)S(1)}, bf16[1,256,2048]{2,1,0:T(8,128)(2,1)}, u32[]{:S(2)}) copy-start(bf16[1,256,2048]{2,1,0:T(8,128)(2,1)} %all-gather.21.cloned.1.call-done) | copy-start | bytes 3145732
  551.8 42.0 %copy-start.1 = (bf16[64,2048]{1,0:T(8,128)(2,1)S(1)}, bf16[64,2048]{1,0:T(8,128)(2,1)}, u32[]{:S(2)}) copy-start(bf16[64,2048]{1,0:T(8,128)(2,1)} %get-tuple-element.27) | copy-start | bytes 786436
Sparse Core Ops, SparseCore 0:
  25.0 14.9 all-gather.8
  41.5 16.7 all-gather.20
  61.2 43.8 reduce-scatter.8
  107.9 43.1 reduce-scatter.6
  153.9 45.2 all-gather.10
  211.2 23.5 reduce-scatter.10
  250.2 13.9 all-gather.16
  265.9 16.7 all-gather.12
  284.3 16.7 all-gather.14
  303.8 54.9 reduce-scatter.14
  361.7 43.1 reduce-scatter.12
  407.7 77.3 all-gather.18
  529.6 23.0 reduce-scatter.16
